TPU v7x, 32 devices: a whole 2x2x4 slice. The times are simulated.
32 devices in a mesh: blk: 16 (over z, x, core), uly: 2 (over y).
Axes of the slice: x: 2, y: 2, z: 4, core: 2. Of those that a mesh axis runs over, the one named last changes fastest.
Arguments:
- tokens: bfloat16 [8192, 1024], P(('blk', 'uly')), may hold values from -32 to 32
- w_qkv: bfloat16 [1024, 3072], replicated, may hold values from -0.1875 to 0.1875
- w_out: bfloat16 [1024, 1024], replicated, may hold values from -0.1875 to 0.1875
- band: int32 [64], P('blk'), may hold values from 1 to 8, as said below
- global_ids: int32 [4], replicated, may hold values from 0 to 63, as said below
Outputs:
- mixed: bfloat16 [8192, 1024], P(('blk', 'uly'))
Inputs may be any that keep to these rules, and one draw needn't show every extreme that they name: `band`: every value from 1 to 8 may occur; both ends occur. `global_ids`: distinct block ids; the first and the last block are among them.
All inputs are finite; a program needn't handle non-finite values.
Results may differ from a plain program's by a relative error of at most 0.007.
The roundings to bfloat16 on the way count: a program that leaves them out, or rounds other values in their place, can miss the bound.
Values may be sent and summed in bfloat16 or wider, within the bound.
A program may use at most 64 MiB of HBM per device.

v0:
```python
import jax
import jax.numpy as jnp
from jax import lax
from jax.sharding import PartitionSpec as P

H = 8
HD = 128
REACH = 2
NGLOBAL = 4


def from_behind(block, axis, distance):
    devices = range(lax.axis_size(axis))
    route = [(i - distance, i) for i in devices if i - distance in devices]
    return lax.ppermute(block, axis, route)


def body(tokens, w_qkv, w_out, band, global_ids):
    tok_dev = tokens.shape[0]
    heads_dev = H // lax.axis_size("uly")
    qkv = jnp.dot(tokens, w_qkv, preferred_element_type=jnp.float32).astype(jnp.bfloat16)
    qkv = qkv.reshape(tok_dev, 3, H, HD)
    regrouped = lax.all_to_all(qkv, "uly", split_axis=2, concat_axis=0, tiled=True)
    context = regrouped.shape[0]
    blocks_dev = context // 128
    queries = regrouped[:, 0]
    key_value = regrouped[:, 1:]
    my_block = lax.axis_index("blk")
    blk_count = lax.axis_size("blk")
    lower_side = []
    upper_side = []
    going_down = key_value
    going_up = key_value
    for offset in range(REACH):
        going_down = from_behind(going_down, "blk", 1)
        going_up = from_behind(going_up, "blk", -1)
        lower_side.append(going_down)
        upper_side.append(going_up)
    banded = jnp.concatenate(lower_side[::-1] + [key_value] + upper_side, 0)
    local_ids = global_ids - my_block * blocks_dev
    picker = (local_ids[:, None] == jnp.arange(blocks_dev, dtype=jnp.int32)[None, :]).astype(
        jnp.bfloat16
    )
    owned = key_value.reshape(blocks_dev, 128 * 2 * heads_dev * HD)
    contrib = jnp.dot(picker, owned, preferred_element_type=jnp.float32)
    gathered = lax.psum(contrib.astype(jnp.bfloat16), "blk")
    gathered = gathered.reshape(NGLOBAL * 128, 2, heads_dev, HD)
    global_keys = gathered[:, 0]
    global_values = gathered[:, 1]
    max_band = REACH * blocks_dev
    window = (2 * max_band + 1) * 128
    total_blocks = blk_count * blocks_dev
    score_scale = 1.0 / HD**0.5

    def attend_block(local_block):
        start = local_block * 128
        q_rows = lax.dynamic_slice_in_dim(queries, start, 128, 0)
        win_pairs = lax.dynamic_slice_in_dim(banded, start, window, 0)
        all_keys = jnp.concatenate([win_pairs[:, 0], global_keys], 0)
        all_values = jnp.concatenate([win_pairs[:, 1], global_values], 0)
        scores = (
            jnp.einsum("qhd,khd->hqk", q_rows, all_keys, preferred_element_type=jnp.float32)
            * score_scale
        )
        q_block = my_block * blocks_dev + local_block
        width_here = band[local_block]
        key_blocks = q_block - max_band + jnp.arange(window, dtype=jnp.int32) // 128
        in_window = (
            (key_blocks >= 0)
            & (key_blocks < total_blocks)
            & (jnp.abs(key_blocks - q_block) <= width_here)
        )
        in_global = jnp.repeat(jnp.abs(global_ids - q_block) > width_here, 128)
        allowed = jnp.concatenate([in_window, in_global])
        scores = jnp.where(allowed[None, None, :], scores, -jnp.inf)
        highest = jnp.max(scores, axis=-1, keepdims=True)
        weights = jnp.exp(scores - highest)
        totals = jnp.sum(weights, axis=-1)
        rounded = weights.astype(jnp.bfloat16)
        result = jnp.einsum("hqk,khd->qhd", rounded, all_values, preferred_element_type=jnp.float32)
        result = result / jnp.transpose(totals)[:, :, None]
        return result.astype(jnp.bfloat16)

    attended = lax.map(attend_block, jnp.arange(blocks_dev, dtype=jnp.int32))
    attended = attended.reshape(context, heads_dev, HD)
    returned = lax.all_to_all(attended, "uly", split_axis=0, concat_axis=1, tiled=True)
    result = jnp.dot(returned.reshape(tok_dev, H * HD), w_out, preferred_element_type=jnp.float32)
    return result.astype(jnp.bfloat16)


def solution(mesh):
    return jax.shard_map(
        body,
        mesh=mesh,
        in_specs=(P(("blk", "uly"), None), P(), P(), P("blk"), P()),
        out_specs=P(("blk", "uly"), None),
        check_vma=False,
    )
```

profile of v0, /device:TPU:0, one launch (start us, length us, event | category | flops | bytes accessed | tf_op | source)
XLA Modules:
  0.0 265.0 jit_solution(4882640663650970089)
XLA Ops:
  6.5 4.9 %fusion.46 = bf16[32,8,24,128]{3,1,2,0:T(8,128)(2,1)S(1)} fusion(bf16[256,1024]{1,0:T(8,128)(2,1)} %param.7, bf16[1024,3072]{1,0:T(8,128)(2,1)} %param.8), kind=kOutput, calls=%fused_computation.43 | convolution fusion | flops 1611399168 | bytes 8388608 | tf_op jit(solution)/shard_map/dot_general | solution.py:21
  12.1 23.2 %all_to_all.33 = bf16[256,3,8,128]{3,0,1,2:T(8,128)(2,1)S(1)} all-to-all(bf16[256,3,8,128]{3,0,1,2:T(8,128)(2,1)S(1)} %copy.32), channel_id=1, replica_groups=mesh['blk'=16,'uly'=2] {'uly'}, dimensions={2} | all-to-all | bytes 3145728 | tf_op jit(solution)/shard_map/all_to_all | solution.py:23
  37.7 2.3 collective-permute-start
  41.3 3.0 %copy.34 = bf16[512,2,4,128]{3,2,1,0:T(4,128)(2,1)} copy(bf16[512,2,4,128]{3,0,2,1:T(8,128)(2,1)} %slice.28) | data formatting | bytes 2097152 | tf_op jit(solution)/shard_map/slice | solution.py:27
  44.4 1.6 reshape.27
  46.0 21.6 %collective-permute-start.1 = (bf16[512,2,4,128]{3,0,2,1:T(8,128)(2,1)}, bf16[512,2,4,128]{3,0,2,1:T(8,128)(2,1)}, u32[]{:S(2)}, u32[]{:S(2)}) collective-permute-start(bf16[512,2,4,128]{3,0,2,1:T(8,128)(2,1)} %collective-permute-done), channel_id=1, source_target_pairs={{0,2},{2,4},{4,6},{6,8},{8,10},{10,12},{12,14},{14,16},{16,18},{18... | collective-permute-start | bytes 3145736 | tf_op jit(solution)/shard_map/ppermute | solution.py:15
  67.6 1.8 convolution_convert_fusion
  69.4 2.3 reshape.28
  72.8 1.3 collective-permute-start.3
  74.1 1.9 slice_bitcast_fusion.1
  76.0 92.1 %all-reduce.2.cloned.1.call-done = bf16[512,2,4,128]{3,0,2,1:T(8,128)(2,1)} async-done(((bf16[512,2,4,128]{3,0,2,1:T(8,128)(2,1)}), bf16[512,2,4,128]{3,0,2,1:T(8,128)(2,1)}) %all-reduce.2.cloned.1.call-update) | async-done | bytes 1048592 | tf_op jit(solution)/shard_map/psum | solution.py:46
  168.1 2.4 slice_bitcast_fusion
  170.5 1.3 constant_dynamic-update-slice_fusion.5
  171.8 1.4 constant_dynamic-update-slice_fusion.4
  173.3 1.4 constant_dynamic-update-slice_fusion.2
  174.9 2.3 copy-done.1
  177.2 67.7 %while.12 = (s32[]{:T(128)}, bf16[4,128,4,128]{3,1,0,2:T(8,128)(2,1)}, s32[4]{0:T(128)S(1)}, bf16[2560,2,4,128]{3,0,2,1:T(8,128)(2,1)}, bf16[512,4,128]{2,0,1:T(...) while((s32[]{:T(128)}, ...), condition=%wide.region_4.5_spmd, body=%wide.region_1.4_spmd.sunk | while | flops 725454464 | bytes 44848596 | solution.py:84
  183.0 4.8 %dynamic-slice_bitcast_fusion.3 = (bf16[2176,4,128]{2,0,1:T(8,128)(2,1)}, bf16[2176,4,128]{2,0,1:T(8,128)(2,1)}) fusion(bf16[2560,2,4,128]{3,0,2,1:T(8,128)(2,1)} %get-tuple-element.269, s32[]{:T(128)S(6)} %select_n.60, s32[]{:T(128)S(6)} %add.89), kind=kLoop, calls=%fused_computation.13.clone.1 | loop fusion | bytes 8912904 | tf_op jit(solution)/shard_map/while/body/eval_jaxpr/squeeze | solution.py:60
  187.8 2.9 %fusion.63 = (f32[4,128]{1,0:T(4,128)S(1)}, f32[4,128,2688]{2,1,0:T(8,128)S(1)}) fusion(bf16[512,4,128]{2,0,1:T(8,128)(2,1)S(1)} %copy-done.5, bf16[2176,4,128]{2,0,1:T(8,128)(2,1)} %get-tuple-element.226, bf16[512,4,128]{2,0,1:T(8,128)(2,1)} %get-tuple-element.274, s32[]{:T(128)S(6)} %select_n.61, pred[2688]{0:T(1024)(128)(4,1)S(1)} %pad_add_fusion.2), kind=kOutput, calls=%fused_computation.56.clone.1 | convolution fusion | flops 361954816 | bytes 8393348 | tf_op jit(solution)/shard_map/while/body/eval_jaxpr/qhd,khd->hqk/dot_general | solution.py:62
  191.5 1.7 fusion.65
  199.9 4.8 %dynamic-slice_bitcast_fusion.3 = (bf16[2176,4,128]{2,0,1:T(8,128)(2,1)}, bf16[2176,4,128]{2,0,1:T(8,128)(2,1)}) fusion(bf16[2560,2,4,128]{3,0,2,1:T(8,128)(2,1)} %get-tuple-element.269, s32[]{:T(128)S(6)} %select_n.60, s32[]{:T(128)S(6)} %add.89), kind=kLoop, calls=%fused_computation.13.clone.1 | loop fusion | bytes 8912904 | tf_op jit(solution)/shard_map/while/body/eval_jaxpr/squeeze | solution.py:60
  204.7 2.9 %fusion.63 = (f32[4,128]{1,0:T(4,128)S(1)}, f32[4,128,2688]{2,1,0:T(8,128)S(1)}) fusion(bf16[512,4,128]{2,0,1:T(8,128)(2,1)S(1)} %copy-done.5, bf16[2176,4,128]{2,0,1:T(8,128)(2,1)} %get-tuple-element.226, bf16[512,4,128]{2,0,1:T(8,128)(2,1)} %get-tuple-element.274, s32[]{:T(128)S(6)} %select_n.61, pred[2688]{0:T(1024)(128)(4,1)S(1)} %pad_add_fusion.2), kind=kOutput, calls=%fused_computation.56.clone.1 | convolution fusion | flops 361954816 | bytes 8393348 | tf_op jit(solution)/shard_map/while/body/eval_jaxpr/qhd,khd->hqk/dot_general | solution.py:62
  208.4 1.7 fusion.65
  216.8 4.8 %dynamic-slice_bitcast_fusion.3 = (bf16[2176,4,128]{2,0,1:T(8,128)(2,1)}, bf16[2176,4,128]{2,0,1:T(8,128)(2,1)}) fusion(bf16[2560,2,4,128]{3,0,2,1:T(8,128)(2,1)} %get-tuple-element.269, s32[]{:T(128)S(6)} %select_n.60, s32[]{:T(128)S(6)} %add.89), kind=kLoop, calls=%fused_computation.13.clone.1 | loop fusion | bytes 8912904 | tf_op jit(solution)/shard_map/while/body/eval_jaxpr/squeeze | solution.py:60
  221.6 2.9 %fusion.63 = (f32[4,128]{1,0:T(4,128)S(1)}, f32[4,128,2688]{2,1,0:T(8,128)S(1)}) fusion(bf16[512,4,128]{2,0,1:T(8,128)(2,1)S(1)} %copy-done.5, bf16[2176,4,128]{2,0,1:T(8,128)(2,1)} %get-tuple-element.226, bf16[512,4,128]{2,0,1:T(8,128)(2,1)} %get-tuple-element.274, s32[]{:T(128)S(6)} %select_n.61, pred[2688]{0:T(1024)(128)(4,1)S(1)} %pad_add_fusion.2), kind=kOutput, calls=%fused_computation.56.clone.1 | convolution fusion | flops 361954816 | bytes 8393348 | tf_op jit(solution)/shard_map/while/body/eval_jaxpr/qhd,khd->hqk/dot_general | solution.py:62
  225.3 1.7 fusion.65
  233.7 4.8 %dynamic-slice_bitcast_fusion.3 = (bf16[2176,4,128]{2,0,1:T(8,128)(2,1)}, bf16[2176,4,128]{2,0,1:T(8,128)(2,1)}) fusion(bf16[2560,2,4,128]{3,0,2,1:T(8,128)(2,1)} %get-tuple-element.269, s32[]{:T(128)S(6)} %select_n.60, s32[]{:T(128)S(6)} %add.89), kind=kLoop, calls=%fused_computation.13.clone.1 | loop fusion | bytes 8912904 | tf_op jit(solution)/shard_map/while/body/eval_jaxpr/squeeze | solution.py:60
  238.5 2.9 %fusion.63 = (f32[4,128]{1,0:T(4,128)S(1)}, f32[4,128,2688]{2,1,0:T(8,128)S(1)}) fusion(bf16[512,4,128]{2,0,1:T(8,128)(2,1)S(1)} %copy-done.5, bf16[2176,4,128]{2,0,1:T(8,128)(2,1)} %get-tuple-element.226, bf16[512,4,128]{2,0,1:T(8,128)(2,1)} %get-tuple-element.274, s32[]{:T(128)S(6)} %select_n.61, pred[2688]{0:T(1024)(128)(4,1)S(1)} %pad_add_fusion.2), kind=kOutput, calls=%fused_computation.56.clone.1 | convolution fusion | flops 361954816 | bytes 8393348 | tf_op jit(solution)/shard_map/while/body/eval_jaxpr/qhd,khd->hqk/dot_general | solution.py:62
  242.3 1.7 fusion.65
  244.8 1.4 copy.37
  246.3 10.0 %all_to_all.34 = bf16[512,4,128]{2,1,0:T(4,128)(2,1)S(1)} all-to-all(bf16[512,4,128]{2,1,0:T(4,128)(2,1)S(1)} %copy.37), channel_id=1, replica_groups=mesh['blk'=16,'uly'=2] {'uly'}, dimensions={0} | all-to-all | bytes 1048576 | tf_op jit(solution)/shard_map/all_to_all | solution.py:86
  256.6 1.5 convolution_convert_fusion.2
  (90 shorter events, 23.4 us)
Async XLA Ops:
  6.5 250.1 %copy-start = (bf16[1024,1024]{1,0:T(8,128)(2,1)S(1)}, bf16[1024,1024]{1,0:T(8,128)(2,1)}, u32[]{:S(2)}) copy-start(bf16[1024,1024]{1,0:T(8,128)(2,1)} %param.9) | copy-start | bytes 6291460
  6.5 161.6 %all-reduce.2.cloned.1.call-start = ((), (), s32[]{:S(2)}) async-start(), calls=%async_computation.2 | async-start | bytes 2097152 | tf_op jit(solution)/shard_map/psum | solution.py:46
  11.8 29.5 %copy-start.7 = (s32[4]{0:T(128)S(1)}, s32[4]{0:T(128)}, u32[]{:S(2)}) copy-start(s32[4]{0:T(128)} %param.11) | copy-start | bytes 52
  35.5 1.2 copy-start.3
  37.7 8.2 %collective-permute-start = (bf16[512,2,4,128]{3,0,2,1:T(8,128)(2,1)}, bf16[512,2,4,128]{3,0,2,1:T(8,128)(2,1)}, u32[]{:S(2)}, u32[]{:S(2)}) collective-permute-start(bf16[512,2,4,128]{3,0,2,1:T(8,128)(2,1)} %slice.28), channel_id=1, source_target_pairs={{0,2},{2,4},{4,6},{6,8},{8,10},{10,12},{12,14},{14,16},{16,18},{18... | collective-permute-start | bytes 3145736 | tf_op jit(solution)/shard_map/ppermute | solution.py:15
  40.0 32.8 %collective-permute-start.2 = (bf16[512,2,4,128]{3,0,2,1:T(8,128)(2,1)}, bf16[512,2,4,128]{3,0,2,1:T(8,128)(2,1)}, u32[]{:S(2)}, u32[]{:S(2)}) collective-permute-start(bf16[512,2,4,128]{3,0,2,1:T(8,128)(2,1)} %slice.28), channel_id=1, source_target_pairs={{2,0},{4,2},{6,4},{8,6},{10,8},{12,10},{14,12},{16,14},{18,16},{20... | collective-permute-start | bytes 3145736 | tf_op jit(solution)/shard_map/ppermute | solution.py:15
  46.0 124.5 %collective-permute-start.1 = (bf16[512,2,4,128]{3,0,2,1:T(8,128)(2,1)}, bf16[512,2,4,128]{3,0,2,1:T(8,128)(2,1)}, u32[]{:S(2)}, u32[]{:S(2)}) collective-permute-start(bf16[512,2,4,128]{3,0,2,1:T(8,128)(2,1)} %collective-permute-done), channel_id=1, source_target_pairs={{0,2},{2,4},{4,6},{6,8},{8,10},{10,12},{12,14},{14,16},{16,18},{18... | collective-permute-start | bytes 3145736 | tf_op jit(solution)/shard_map/ppermute | solution.py:15
  72.8 101.9 %collective-permute-start.3 = (bf16[512,2,4,128]{3,0,2,1:T(8,128)(2,1)}, bf16[512,2,4,128]{3,0,2,1:T(8,128)(2,1)S(1)}, u32[]{:S(2)}, u32[]{:S(2)}) collective-permute-start(bf16[512,2,4,128]{3,0,2,1:T(8,128)(2,1)} %collective-permute-done.2), channel_id=1, source_target_pairs={{2,0},{4,2},{6,4},{8,6},{10,8},{12,10},{14,12},{16,14},{18,16},{20... | collective-permute-start | bytes 3145736 | tf_op jit(solution)/shard_map/ppermute | solution.py:15
  168.1 5.1 %copy-start.4 = (bf16[2,256,3,4,128]{4,1,0,3,2:T(8,128)(2,1)S(1)}, bf16[2,256,3,4,128]{4,1,0,3,2:T(8,128)(2,1)}, u32[]{:S(2)}) copy-start(bf16[2,256,3,4,128]{4,1,0,3,2:T(8,128)(2,1)} %copy-done.3) | copy-start | bytes 4718596
  170.5 6.7 %copy-start.8 = (s32[4]{0:T(128)S(1)}, s32[4]{0:T(128)}, u32[]{:S(2)}) copy-start(s32[4]{0:T(128)} %param.10) | copy-start | bytes 52
  174.9 2.3 copy-start.1
  177.2 10.6 %copy-start.5 = (bf16[512,4,128]{2,0,1:T(8,128)(2,1)S(1)}, bf16[512,4,128]{2,0,1:T(8,128)(2,1)}, u32[]{:S(2)}) copy-start(bf16[512,4,128]{2,0,1:T(8,128)(2,1)} %get-tuple-element.275) | copy-start | bytes 1572868 | tf_op jit(solution)/shard_map/while
  187.7 3.8 %copy-start.2 = (bf16[2176,4,128]{2,0,1:T(8,128)(2,1)S(1)}, bf16[2176,4,128]{2,0,1:T(8,128)(2,1)}, u32[]{:S(2)}) copy-start(bf16[2176,4,128]{2,0,1:T(8,128)(2,1)} %get-tuple-element.229) | copy-start | bytes 6684676 | tf_op jit(solution)/shard_map/while
  187.7 3.8 %copy-start.6 = (bf16[512,4,128]{2,0,1:T(8,128)(2,1)S(1)}, bf16[512,4,128]{2,0,1:T(8,128)(2,1)}, u32[]{:S(2)}) copy-start(bf16[512,4,128]{2,0,1:T(8,128)(2,1)} %get-tuple-element.270) | copy-start | bytes 1572868 | tf_op jit(solution)/shard_map/while
  194.1 10.6 %copy-start.5 = (bf16[512,4,128]{2,0,1:T(8,128)(2,1)S(1)}, bf16[512,4,128]{2,0,1:T(8,128)(2,1)}, u32[]{:S(2)}) copy-start(bf16[512,4,128]{2,0,1:T(8,128)(2,1)} %get-tuple-element.275) | copy-start | bytes 1572868 | tf_op jit(solution)/shard_map/while
  204.7 3.7 %copy-start.2 = (bf16[2176,4,128]{2,0,1:T(8,128)(2,1)S(1)}, bf16[2176,4,128]{2,0,1:T(8,128)(2,1)}, u32[]{:S(2)}) copy-start(bf16[2176,4,128]{2,0,1:T(8,128)(2,1)} %get-tuple-element.229) | copy-start | bytes 6684676 | tf_op jit(solution)/shard_map/while
  204.7 3.8 %copy-start.6 = (bf16[512,4,128]{2,0,1:T(8,128)(2,1)S(1)}, bf16[512,4,128]{2,0,1:T(8,128)(2,1)}, u32[]{:S(2)}) copy-start(bf16[512,4,128]{2,0,1:T(8,128)(2,1)} %get-tuple-element.270) | copy-start | bytes 1572868 | tf_op jit(solution)/shard_map/while
  211.0 10.6 %copy-start.5 = (bf16[512,4,128]{2,0,1:T(8,128)(2,1)S(1)}, bf16[512,4,128]{2,0,1:T(8,128)(2,1)}, u32[]{:S(2)}) copy-start(bf16[512,4,128]{2,0,1:T(8,128)(2,1)} %get-tuple-element.275) | copy-start | bytes 1572868 | tf_op jit(solution)/shard_map/while
  221.6 3.7 %copy-start.2 = (bf16[2176,4,128]{2,0,1:T(8,128)(2,1)S(1)}, bf16[2176,4,128]{2,0,1:T(8,128)(2,1)}, u32[]{:S(2)}) copy-start(bf16[2176,4,128]{2,0,1:T(8,128)(2,1)} %get-tuple-element.229) | copy-start | bytes 6684676 | tf_op jit(solution)/shard_map/while
  221.6 3.8 %copy-start.6 = (bf16[512,4,128]{2,0,1:T(8,128)(2,1)S(1)}, bf16[512,4,128]{2,0,1:T(8,128)(2,1)}, u32[]{:S(2)}) copy-start(bf16[512,4,128]{2,0,1:T(8,128)(2,1)} %get-tuple-element.270) | copy-start | bytes 1572868 | tf_op jit(solution)/shard_map/while
  227.9 10.6 %copy-start.5 = (bf16[512,4,128]{2,0,1:T(8,128)(2,1)S(1)}, bf16[512,4,128]{2,0,1:T(8,128)(2,1)}, u32[]{:S(2)}) copy-start(bf16[512,4,128]{2,0,1:T(8,128)(2,1)} %get-tuple-element.275) | copy-start | bytes 1572868 | tf_op jit(solution)/shard_map/while
  238.5 3.7 %copy-start.2 = (bf16[2176,4,128]{2,0,1:T(8,128)(2,1)S(1)}, bf16[2176,4,128]{2,0,1:T(8,128)(2,1)}, u32[]{:S(2)}) copy-start(bf16[2176,4,128]{2,0,1:T(8,128)(2,1)} %get-tuple-element.229) | copy-start | bytes 6684676 | tf_op jit(solution)/shard_map/while
  238.5 3.8 %copy-start.6 = (bf16[512,4,128]{2,0,1:T(8,128)(2,1)S(1)}, bf16[512,4,128]{2,0,1:T(8,128)(2,1)}, u32[]{:S(2)}) copy-start(bf16[512,4,128]{2,0,1:T(8,128)(2,1)} %get-tuple-element.270) | copy-start | bytes 1572868 | tf_op jit(solution)/shard_map/while
Sparse Core Ops, SparseCore 0:
  72.9 95.1 all-reduce.1
where the time goes:
time: 266 us; the launch traced here: 265 us
  waiting for transfers between devices  92.2 us (35%)
  local copies, waits for them, and re-layouts  51.2 us (19%)
  blocking collectives  33.3 us (13%)
  starting transfers between devices  26.5 us (10%)
  matrix products  26.5 us (10%)
  between operations  13.6 us (5%)
  loops' own time  13 us (5%)
  other arithmetic  8.73 us (3%)
    psum x1, waiting for transfers between devices, body(): gathered = lax.psum(contrib.astype(jnp.bfloat16), 'blk')  92.1 us
    ppermute x4, starting transfers between devices, from_behind(): return lax.ppermute(block, axis, route)  26.5 us
    all_to_all x1, blocking collectives, body(): lax.all_to_all(qkv, 'uly', split_axis=2, concat_axis=0, tiled=True)  23.2 us
    squeeze x4, local copies, waits for them, and re-layouts, attend_block(): all_values = jnp.concatenate([win_pairs[:, 1], global_values], 0)  19 us
    another operation x1, loops' own time, body(): attended = lax.map(attend_block, jnp.arange(blocks_dev, dtype=jnp.int32))  13 us
    dot_general x4, matrix products, attend_block(): jnp.einsum('qhd,khd->hqk', q_rows, all_keys, preferred_element_type=jnp.f...  11.4 us
    all_to_all x1, blocking collectives, body(): lax.all_to_all(attended, 'uly', split_axis=0, concat_axis=1, tiled=True)  10 us
    unnamed x17, local copies, waits for them, and re-layouts  7.92 us
  transfers between devices with their start and end apart: 5, of which 1 were waited for; matrix products, arithmetic and copies ran while one was open for 7% of the time, Pallas kernels for 0%

commit v1 on v0

v1 whole, which is shorter than its diff:
```python
import functools
import math

import jax
import jax.numpy as jnp
from jax import lax
from jax.experimental import pallas as pl
from jax.experimental.pallas import tpu as pltpu
from jax.sharding import PartitionSpec as P

H = 8
HD = 128
BLOCK = 128
NGLOBAL = 4
REACH = 2
SLOTS = 2 * REACH + 1
VMEM_LIMIT = 56 * 1024 * 1024
EXP2_SCALE = math.log2(math.e) / HD**0.5
MASKED = -1e30


def gather_kernel(
    nb, nu, ids_ref, tok_ref, w_ref, q_ref, win_ref, glob_ref,
    qkv_ref, own_ref, pre_ref, suf_ref, up_ref, down_ref,
    a2a_s, a2a_r, x_s, x_r, c_s, c_r, f_s, f_r, z_s, z_r,
    up_s, up_r, dn_s, dn_r, gx_s, gx_r, gc_s, gc_r, gf_s, gf_r,
):
    tok = tok_ref.shape[0]
    hd = H // nu
    ctx = tok * nu
    bd = ctx // BLOCK
    nz = nb // 4
    half = NGLOBAL // 2
    nj = 2 * hd
    b = lax.axis_index("blk")
    u = lax.axis_index("uly")
    r = b % 4
    z = b // 4
    low = r < 2
    inner = (r == 1) | (r == 2)
    has_up = z < nz - 1
    has_dn = z > 0
    px = jnp.where(low, b + 2, b - 2)
    pc = jnp.where(r % 2 == 0, b + 1, b - 1)

    barrier = pltpu.get_barrier_semaphore()

    def greet(blk, uly):
        pl.semaphore_signal(
            barrier, inc=1, device_id=(blk, uly), device_id_type=pl.DeviceIdType.MESH
        )

    for d in range(1, nu):
        greet(b, (u + d) % nu)
    greet(px, u)
    greet(pc, u)
    pl.when(has_up)(lambda: greet(b + 4, u))
    pl.when(has_dn)(lambda: greet(b - 4, u))
    pl.semaphore_wait(
        barrier, nu + 1 + jnp.where(has_up, 1, 0) + jnp.where(has_dn, 1, 0)
    )

    def rdma(src, dst, s, rr, blk, uly):
        return pltpu.make_async_remote_copy(
            src_ref=src, dst_ref=dst, send_sem=s, recv_sem=rr,
            device_id=(blk, uly), device_id_type=pl.DeviceIdType.MESH,
        )

    def slot(j, s):
        return win_ref.at[j, pl.ds(pl.multiple_of(s * ctx, ctx), ctx)]

    def clear(s):
        win_ref[:, pl.ds(s * ctx, ctx), :] = jnp.zeros((nj, ctx, HD), jnp.bfloat16)

    pl.when(b < 2)(lambda: clear(0))
    pl.when(b < 1)(lambda: clear(1))
    pl.when(b > nb - 2)(lambda: clear(3))
    pl.when(b > nb - 3)(lambda: clear(4))

    def a2a(d, j, part, h):
        to = (u + d) % nu
        rows = pl.ds(pl.multiple_of(u * tok, tok), tok)
        if part == 0:
            dst = q_ref.at[h, rows]
        else:
            dst = win_ref.at[
                (part - 1) * hd + h, pl.ds(pl.multiple_of(2 * ctx + u * tok, tok), tok)
            ]
        return rdma(
            qkv_ref.at[part * H + to * hd + h], dst,
            a2a_s.at[d - 1, j], a2a_r.at[d - 1, j], b, to,
        )

    def chunks(part):
        return [(j, j - {1: 0, 2: hd, 0: 2 * hd}[part])
                for j in range({1: 0, 2: hd, 0: 2 * hd}[part], {1: hd, 2: 2 * hd, 0: 3 * hd}[part])]

    for part in (1, 2, 0):
        for p in range(H // 2):
            col = part * H * HD + p * 2 * HD
            res = jnp.dot(
                tok_ref[...], w_ref[:, col:col + 2 * HD], preferred_element_type=jnp.float32
            ).astype(jnp.bfloat16)
            qkv_ref[part * H + 2 * p] = res[:, :HD]
            qkv_ref[part * H + 2 * p + 1] = res[:, HD:]
        for j, h in chunks(part):
            for d in range(1, nu):
                a2a(d, j, part, h).start()
        for j, h in chunks(part):
            mine = qkv_ref[part * H + u * hd + h]
            if part == 0:
                q_ref[h, pl.ds(pl.multiple_of(u * tok, tok), tok)] = mine
            else:
                win_ref[j, pl.ds(pl.multiple_of(2 * ctx + u * tok, tok), tok)] = mine

    s_x = jnp.where(low, 0, 4)
    s_c = jnp.where(r % 2 == 0, 1, 3)
    in_x = 4 - s_x
    f_src = jnp.where((r == 0) | (r == 2), 4, 0)
    f_dst = jnp.where((r == 0) | (r == 2), 3, 1)

    def x_copy(j):
        return rdma(slot(j, 2), slot(j, s_x), x_s.at[j], x_r.at[j], px, u)

    def c_copy(j):
        return rdma(slot(j, 2), slot(j, s_c), c_s.at[j], c_r.at[j], pc, u)

    def f_copy(j):
        return rdma(slot(j, f_src), slot(j, f_dst), f_s.at[j], f_r.at[j], pc, u)

    z_to = jnp.where(low, b + 4, b - 4)
    z_sends = (low & has_up) | (~low & has_dn)
    z_gets = (low & has_dn) | (~low & has_up)
    f_sends = (r == 0) | (r == 3) | z_gets
    f_gets = inner | z_gets

    def z_copy(j):
        return rdma(slot(j, in_x), slot(j, s_x), z_s.at[j], z_r.at[j], z_to, u)

    def stage_a(j):
        part = 1 + j // hd
        for d in range(1, nu):
            a2a(d, j, part, j % hd).wait_recv()
        x_copy(j).start()
        c_copy(j).start()

    def stage_b(j):
        x_copy(j).wait_recv()
        pl.when((r == 0) | (r == 3))(lambda: f_copy(j).start())
        pl.when(z_sends)(lambda: z_copy(j).start())

    def stage_c(j):
        @pl.when(z_gets)
        def _():
            z_copy(j).wait_recv()
            pl.when(inner)(lambda: f_copy(j).start())
        c_copy(j).wait_recv()

        @pl.when(inner)
        def _():
            f_copy(j).wait_recv()
            first = jnp.where(r == 1, 1, 0)
            for g in range(half):
                gid = jnp.where(r == 1, ids_ref[g], ids_ref[half + g]) - 4 * z * bd

                def add(i, acc):
                    blk = win_ref[j, pl.ds(pl.multiple_of((first * bd + i) * BLOCK, BLOCK), BLOCK)]
                    take = jnp.where(gid == i, 1.0, 0.0).astype(jnp.float32)
                    return acc + blk.astype(jnp.float32) * take

                acc = lax.fori_loop(0, 4 * bd, add, jnp.zeros((BLOCK, HD), jnp.float32))
                own_ref[j, g * BLOCK:(g + 1) * BLOCK] = acc.astype(jnp.bfloat16)

    def up_copy(j):
        return rdma(up_ref.at[j], pre_ref.at[j], up_s.at[j], up_r.at[j], b + 4, u)

    def dn_copy(j):
        return rdma(down_ref.at[j], suf_ref.at[j], dn_s.at[j], dn_r.at[j], b - 4, u)

    def wait_in(kind, other, sem_s, sem_r, j):
        rdma(kind.at[j], kind.at[j], sem_s.at[j], sem_r.at[j], other, u).wait_recv()

    def stage_up(j):
        @pl.when(inner)
        def _():
            @pl.when(has_dn)
            def _():
                wait_in(pre_ref, b - 4, up_s, up_r, j)

            @pl.when(~has_dn)
            def _():
                pre_ref[j] = jnp.zeros((half * BLOCK, HD), jnp.bfloat16)

            @pl.when(has_up)
            def _():
                up_ref[j] = pre_ref[j] + own_ref[j]
                up_copy(j).start()

    a_half = pl.ds(0, half * BLOCK)
    b_half = pl.ds(half * BLOCK, half * BLOCK)
    mine_half = pl.ds(pl.multiple_of(jnp.where(r == 1, 0, half * BLOCK), BLOCK), half * BLOCK)
    fwd_half = pl.ds(pl.multiple_of(jnp.where(r == 0, half * BLOCK, 0), BLOCK), half * BLOCK)

    def gx_copy(j):
        return rdma(glob_ref.at[j, mine_half], glob_ref.at[j, mine_half],
                    gx_s.at[j], gx_r.at[j], px, u)

    def gc_copy(j):
        return rdma(glob_ref.at[j, mine_half], glob_ref.at[j, mine_half],
                    gc_s.at[j], gc_r.at[j], pc, u)

    def gf_copy(j):
        return rdma(glob_ref.at[j, fwd_half], glob_ref.at[j, fwd_half],
                    gf_s.at[j], gf_r.at[j], pc, u)

    def stage_down(j):
        @pl.when(inner)
        def _():
            @pl.when(has_up)
            def _():
                wait_in(suf_ref, b + 4, dn_s, dn_r, j)

            @pl.when(~has_up)
            def _():
                suf_ref[j] = jnp.zeros((half * BLOCK, HD), jnp.bfloat16)

            total = suf_ref[j] + own_ref[j]

            @pl.when(has_dn)
            def _():
                down_ref[j] = total
                dn_copy(j).start()

            glob_ref[j, mine_half] = total + pre_ref[j]
            gx_copy(j).start()
            gc_copy(j).start()

    def stage_out(j):
        @pl.when(~inner)
        def _():
            gx_copy(j).wait_recv()
            gf_copy(j).start()

    stages = [(0, stage_a), (1, stage_b), (2, stage_c), (3, stage_up), (5, stage_down), (6, stage_out)]
    for t in range(nj + 6):
        for lag, stage in stages:
            if 0 <= t - lag < nj:
                stage(t - lag)

    for part in (1, 2, 0):
        for j, h in chunks(part):
            for d in range(1, nu):
                a2a(d, j, part, h).wait_send()
                if part == 0:
                    a2a(d, j, part, h).wait_recv()
    for j in range(nj):
        x_copy(j).wait_send()
        c_copy(j).wait_send()
        pl.when(f_sends)(lambda: f_copy(j).wait_send())
        pl.when(z_sends)(lambda: z_copy(j).wait_send())
        pl.when(f_gets & ~inner)(lambda: f_copy(j).wait_recv())

        @pl.when(inner)
        def _():
            pl.when(has_up)(lambda: up_copy(j).wait_send())
            pl.when(has_dn)(lambda: dn_copy(j).wait_send())
            gx_copy(j).wait_send()
            gc_copy(j).wait_send()
            gf_copy(j).wait_recv()

        @pl.when(~inner)
        def _():
            gc_copy(j).wait_recv()
            gf_copy(j).wait_send()


def gather(nb, nu, global_ids, tokens, w_qkv):
    tok = tokens.shape[0]
    hd = H // nu
    ctx = tok * nu
    nj = 2 * hd
    part = pltpu.VMEM((nj, NGLOBAL // 2 * BLOCK, HD), jnp.bfloat16)
    dma = pltpu.SemaphoreType.DMA
    vmem = pl.BlockSpec(memory_space=pltpu.VMEM)
    return pl.pallas_call(
        functools.partial(gather_kernel, nb, nu),
        out_shape=[
            jax.ShapeDtypeStruct((hd, ctx, HD), jnp.bfloat16),
            jax.ShapeDtypeStruct((nj, SLOTS * ctx, HD), jnp.bfloat16),
            jax.ShapeDtypeStruct((nj, NGLOBAL * BLOCK, HD), jnp.bfloat16),
        ],
        in_specs=[pl.BlockSpec(memory_space=pltpu.SMEM), vmem, vmem],
        out_specs=[vmem, vmem, vmem],
        scratch_shapes=[
            pltpu.VMEM((3 * H, tok, HD), jnp.bfloat16), part, part, part, part, part,
            dma((nu - 1, 3 * hd)), dma((nu - 1, 3 * hd)),
        ] + [dma((nj,))] * 18,
        compiler_params=pltpu.CompilerParams(
            collective_id=0, has_side_effects=True, vmem_limit_bytes=VMEM_LIMIT
        ),
    )(global_ids, tokens, w_qkv)


def attend_kernel(nb, nu, band_ref, ids_ref, q_ref, win_ref, glob_ref, out_ref):
    hd = H // nu
    ctx = q_ref.shape[1]
    bd = ctx // BLOCK
    reach = REACH * bd
    window = (2 * reach + 1) * BLOCK
    b = lax.axis_index("blk")
    nt = (((1,), (1,)), ((), ()))

    @pl.loop(0, bd)
    def _(lb):
        q_block = b * bd + lb
        width = band_ref[lb]
        key = q_block - reach + lax.broadcasted_iota(jnp.int32, (1, window), 1) // BLOCK
        seen = (jnp.abs(key - q_block) <= width) & (key >= 0) & (key < nb * bd)
        bias_w = jnp.where(seen, 0.0, MASKED)
        lane = lax.broadcasted_iota(jnp.int32, (1, NGLOBAL * BLOCK), 1) // BLOCK
        gid = jnp.zeros_like(lane)
        for g in range(NGLOBAL):
            gid = jnp.where(lane == g, ids_ref[g], gid)
        bias_g = jnp.where(jnp.abs(gid - q_block) > width, 0.0, MASKED)
        rows = pl.ds(pl.multiple_of(lb * BLOCK, BLOCK), BLOCK)
        wrows = pl.ds(pl.multiple_of(lb * BLOCK, BLOCK), window)
        for h in range(hd):
            q = q_ref[h, rows]
            sw = lax.dot_general(q, win_ref[h, wrows], nt, preferred_element_type=jnp.float32)
            sg = lax.dot_general(q, glob_ref[h], nt, preferred_element_type=jnp.float32)
            sw = sw * EXP2_SCALE + bias_w
            sg = sg * EXP2_SCALE + bias_g
            top = jnp.maximum(
                jnp.max(sw, axis=1, keepdims=True), jnp.max(sg, axis=1, keepdims=True)
            )
            pw = jnp.exp2(sw - top)
            pg = jnp.exp2(sg - top)
            total = jnp.sum(pw, axis=1, keepdims=True) + jnp.sum(pg, axis=1, keepdims=True)
            acc = jnp.dot(
                pw.astype(jnp.bfloat16), win_ref[hd + h, wrows], preferred_element_type=jnp.float32
            ) + jnp.dot(
                pg.astype(jnp.bfloat16), glob_ref[hd + h], preferred_element_type=jnp.float32
            )
            out_ref[rows, h * HD:(h + 1) * HD] = (acc / total).astype(jnp.bfloat16)


def attend(nb, nu, band, global_ids, q, win, glob):
    hd, ctx, _ = q.shape
    smem = pl.BlockSpec(memory_space=pltpu.SMEM)
    vmem = pl.BlockSpec(memory_space=pltpu.VMEM)
    return pl.pallas_call(
        functools.partial(attend_kernel, nb, nu),
        out_shape=jax.ShapeDtypeStruct((ctx, hd * HD), jnp.bfloat16),
        in_specs=[smem, smem, vmem, vmem, vmem],
        out_specs=vmem,
        compiler_params=pltpu.CompilerParams(vmem_limit_bytes=VMEM_LIMIT),
    )(band, global_ids, q, win, glob)


def body(nb, nu, tokens, w_qkv, w_out, band, global_ids):
    q, win, glob = gather(nb, nu, global_ids, tokens, w_qkv)
    attended = attend(nb, nu, band, global_ids, q, win, glob)
    returned = lax.all_to_all(attended, "uly", split_axis=0, concat_axis=1, tiled=True)
    result = jnp.dot(returned, w_out, preferred_element_type=jnp.float32)
    return result.astype(jnp.bfloat16)


def solution(mesh):
    return jax.shard_map(
        functools.partial(body, mesh.shape["blk"], mesh.shape["uly"]),
        mesh=mesh,
        in_specs=(P(("blk", "uly"), None), P(), P(), P("blk"), P()),
        out_specs=P(("blk", "uly"), None),
        check_vma=False,
    )
```

time: 266 us -> 192 us (0.72)
  Pallas kernels: 0 us -> 177 us
  waiting for transfers between devices: 92.2 us -> 0 us
  local copies, waits for them, and re-layouts: 51.2 us -> 1.25 us
  starting transfers between devices: 26.5 us -> 0 us
  matrix products: 26.5 us -> 1.52 us
  blocking collectives: 33.3 us -> 11.2 us
  between operations: 13.6 us -> 0.02 us
  loops' own time: 13 us -> 0 us
  other arithmetic: 8.73 us -> 0 us
    pallas_call x0 -> x2, Pallas kernels: none -> 177 us  [the longest x1 163 us: gather(): pl.pallas_call(functools.partial(gather_kernel, nb, nu), out_shape=[jax.S...]
    psum x1 -> x0, waiting for transfers between devices: 92.1 us -> none  [body(): gathered = lax.psum(contrib.astype(jnp.bfloat16), 'blk')]
    ppermute x4 -> x0, starting transfers between devices: 26.5 us -> none  [from_behind(): return lax.ppermute(block, axis, route)]
    dot_general x11 -> x1, matrix products: 26.5 us -> 1.52 us  [body(): result = jnp.dot(returned, w_out, preferred_element_type=jnp.float32)]
    all_to_all x1 -> x0, blocking collectives: 23.2 us -> none  [body(): lax.all_to_all(qkv, 'uly', split_axis=2, concat_axis=0, tiled=True)]
    squeeze x6 -> x0, local copies, waits for them, and re-layouts: 23.2 us -> none  [the longest x4 19 us: attend_block(): all_values = jnp.concatenate([win_pairs[:, 1], global_values], 0)]
    another operation x1 -> x0, loops' own time: 13 us -> none  [body(): attended = lax.map(attend_block, jnp.arange(blocks_dev, dtype=jnp.int32))]
    unnamed x17 -> x2, local copies, waits for them, and re-layouts: 7.92 us -> 0.01 us
  transfers between devices with their start and end apart: 5 -> 0, of which waited for: 1 -> 0; matrix products, arithmetic and copies ran while one was open for 7% -> 0% of each run, Pallas kernels for 0% -> 0%
where the time goes in v1:
time: 192 us; the launch traced here: 191 us
  Pallas kernels  177 us (92%)
  blocking collectives  11.2 us (6%)
    pallas_call x1, Pallas kernels, gather(): pl.pallas_call(functools.partial(gather_kernel, nb, nu), out_shape=[jax.S...  163 us
    pallas_call x1, Pallas kernels, attend(): pl.pallas_call(functools.partial(attend_kernel, nb, nu), out_shape=jax.Sh...  14.8 us
    all_to_all x1, blocking collectives, body(): lax.all_to_all(attended, 'uly', split_axis=0, concat_axis=1, tiled=True)  11.2 us

profile of v1, /device:TPU:0, one launch (start us, length us, event | category | flops | bytes accessed | tf_op | source)
XLA Modules:
  0.0 191.3 jit_solution(904288555148221033)
XLA Ops:
  0.0 0.0 copy-start
  0.0 162.6 %shard_map.55 = (bf16[4,512,128]{2,1,0:T(8,128)(2,1)}, bf16[8,2560,128]{2,1,0:T(8,128)(2,1)}, bf16[8,512,128]{2,1,0:T(8,128)(2,1)}) custom-call(s32[4]{0:T(128)} %ids_ref.3, bf16[256,1024]{1,0:T(8,128)(2,1)} %tok_ref.1, bf16[1024,3072]{1,0:T(8,128)(2,1)} %w_ref.1), custom_call_target="tpu_custom_call" | custom-call | tf_op jit(solution)/shard_map/pallas_call | solution.py:285
  162.6 14.8 %shard_map.56 = bf16[512,512]{1,0:T(8,128)(2,1)} custom-call(s32[4]{0:T(128)} %band_ref.1, s32[4]{0:T(128)} %ids_ref.3, bf16[4,512,128]{2,1,0:T(8,128)(2,1)} %get-tuple-element.8.q_ref, bf16[8,2560,128]{2,1,0:T(8,128)(2,1)} %get-tuple-element.9.win_ref, bf16[8,512,128]{2,1,0:T(8,128)(2,1)} %get-tuple-element.10.glob_ref), custom_call_target="tpu_custom_call" | custom-call | tf_op jit(solution)/shard_map/pallas_call | solution.py:351
  177.4 1.2 copy.6
  178.6 11.2 %all_to_all.19 = bf16[2,256,512]{1,2,0:T(8,128)(2,1)S(1)} all-to-all(bf16[2,256,512]{1,2,0:T(8,128)(2,1)S(1)} %copy.6), channel_id=1, replica_groups=mesh['blk'=16,'uly'=2] {'uly'}, dimensions={0} | all-to-all | bytes 1048576 | tf_op jit(solution)/shard_map/all_to_all | solution.py:363
  189.8 0.0 copy-done
  189.8 1.5 convolution_convert_fusion
Async XLA Ops:
  0.0 189.8 %copy-start = (bf16[1024,1024]{1,0:T(8,128)(2,1)S(1)}, bf16[1024,1024]{1,0:T(8,128)(2,1)}, u32[]{:S(2)}) copy-start(bf16[1024,1024]{1,0:T(8,128)(2,1)} %param.7) | copy-start | bytes 6291460

commit v2 on v1

--- a/solution.py
+++ b/solution.py
@@ -224,14 +224,16 @@
             def _():
                 suf_ref[j] = jnp.zeros((half * BLOCK, HD), jnp.bfloat16)
 
-            total = suf_ref[j] + own_ref[j]
+            down_ref[j] = suf_ref[j] + own_ref[j]
 
             @pl.when(has_dn)
             def _():
-                down_ref[j] = total
                 dn_copy(j).start()
 
-            glob_ref[j, mine_half] = total + pre_ref[j]
+    def stage_spread(j):
+        @pl.when(inner)
+        def _():
+            glob_ref[j, mine_half] = down_ref[j] + pre_ref[j]
             gx_copy(j).start()
             gc_copy(j).start()
 
@@ -241,9 +243,18 @@
             gx_copy(j).wait_recv()
             gf_copy(j).start()
 
-    stages = [(0, stage_a), (1, stage_b), (2, stage_c), (3, stage_up), (5, stage_down), (6, stage_out)]
-    for t in range(nj + 6):
-        for lag, stage in stages:
+    def sweep(j, stage):
+        pl.when((j >= 0) & (j < nj))(lambda: stage(j))
+
+    stages = [(0, stage_a), (1, stage_b), (2, stage_c), (2 + nz, stage_spread), (3 + nz, stage_out)]
+    for t in range(nj + 3 + nz):
+        for lag, stage in stages[:3]:
+            if 0 <= t - lag < nj:
+                stage(t - lag)
+        if t >= 2:
+            sweep(t - 2 - z, stage_up)
+            sweep(t - 2 - (nz - 1 - z), stage_down)
+        for lag, stage in stages[3:]:
             if 0 <= t - lag < nj:
                 stage(t - lag)
 

time: 192 us -> 94.1 us (0.49)
  Pallas kernels: 177 us -> 79.6 us
    pallas_call x1, Pallas kernels: 163 us -> 64.9 us  [gather(): pl.pallas_call(functools.partial(gather_kernel, nb, nu), out_shape=[jax.S...]
where the time goes in v2:
time: 94.1 us; the launch traced here: 93.9 us
  Pallas kernels  79.6 us (85%)
  blocking collectives  11.5 us (12%)
  matrix products  1.52 us (2%)
  local copies, waits for them, and re-layouts  1.25 us (1%)
    pallas_call x1, Pallas kernels, gather(): pl.pallas_call(functools.partial(gather_kernel, nb, nu), out_shape=[jax.S...  64.9 us
    pallas_call x1, Pallas kernels, attend(): pl.pallas_call(functools.partial(attend_kernel, nb, nu), out_shape=jax.Sh...  14.8 us
    all_to_all x1, blocking collectives, body(): lax.all_to_all(attended, 'uly', split_axis=0, concat_axis=1, tiled=True)  11.5 us

profile of v2, /device:TPU:0, one launch (start us, length us, event | category | flops | bytes accessed | tf_op | source)
XLA Modules:
  0.0 93.9 jit_solution(5245016430276952842)
XLA Ops:
  0.0 0.0 copy-start
  0.0 64.9 %shard_map.55 = (bf16[4,512,128]{2,1,0:T(8,128)(2,1)}, bf16[8,2560,128]{2,1,0:T(8,128)(2,1)}, bf16[8,512,128]{2,1,0:T(8,128)(2,1)}) custom-call(s32[4]{0:T(128)} %ids_ref.3, bf16[256,1024]{1,0:T(8,128)(2,1)} %tok_ref.1, bf16[1024,3072]{1,0:T(8,128)(2,1)} %w_ref.1), custom_call_target="tpu_custom_call" | custom-call | tf_op jit(solution)/shard_map/pallas_call | solution.py:296
  64.9 14.8 %shard_map.56 = bf16[512,512]{1,0:T(8,128)(2,1)} custom-call(s32[4]{0:T(128)} %band_ref.1, s32[4]{0:T(128)} %ids_ref.3, bf16[4,512,128]{2,1,0:T(8,128)(2,1)} %get-tuple-element.8.q_ref, bf16[8,2560,128]{2,1,0:T(8,128)(2,1)} %get-tuple-element.9.win_ref, bf16[8,512,128]{2,1,0:T(8,128)(2,1)} %get-tuple-element.10.glob_ref), custom_call_target="tpu_custom_call" | custom-call | tf_op jit(solution)/shard_map/pallas_call | solution.py:362
  79.7 1.2 %copy.6 = bf16[2,256,512]{1,2,0:T(8,128)(2,1)S(1)} copy(bf16[2,256,512]{2,1,0:T(8,128)(2,1)} %bitcast.7) | data formatting | bytes 1048576 | tf_op jit(solution)/shard_map/all_to_all | solution.py:374
  80.9 11.5 %all_to_all.19 = bf16[2,256,512]{1,2,0:T(8,128)(2,1)S(1)} all-to-all(bf16[2,256,512]{1,2,0:T(8,128)(2,1)S(1)} %copy.6), channel_id=1, replica_groups=mesh['blk'=16,'uly'=2] {'uly'}, dimensions={0} | all-to-all | bytes 1048576 | tf_op jit(solution)/shard_map/all_to_all | solution.py:374
  92.4 0.0 copy-done
  92.4 1.5 %convolution_convert_fusion = bf16[256,1024]{1,0:T(8,128)(2,1)} fusion(bf16[256,1024]{0,1:T(8,128)(2,1)S(1)} %bitcast.6, bf16[1024,1024]{1,0:T(8,128)(2,1)S(1)} %copy-done), kind=kOutput, calls=%fused_computation | convolution fusion | flops 537133056 | bytes 3145728 | tf_op jit(solution)/shard_map/dot_general | solution.py:375
Async XLA Ops:
  0.0 92.4 %copy-start = (bf16[1024,1024]{1,0:T(8,128)(2,1)S(1)}, bf16[1024,1024]{1,0:T(8,128)(2,1)}, u32[]{:S(2)}) copy-start(bf16[1024,1024]{1,0:T(8,128)(2,1)} %param.7) | copy-start | bytes 6291460

commit v3 on v2

v3 whole, which is shorter than its diff:
```python
import functools
import math

import jax
import jax.numpy as jnp
from jax import lax
from jax.experimental import pallas as pl
from jax.experimental.pallas import tpu as pltpu
from jax.sharding import PartitionSpec as P

H = 8
HD = 128
BLOCK = 128
NGLOBAL = 4
REACH = 2
SLOTS = 2 * REACH + 1
VMEM_LIMIT = 56 * 1024 * 1024
EXP2_SCALE = math.log2(math.e) / HD**0.5
MASKED = -1e30


def layer_kernel(
    nb, nu, band_ref, ids_ref, tok_ref, w_ref, out_ref,
    q_ref, win_ref, glob_ref, far_ref, wbuf_ref, acc_ref, top_ref, sum_ref, att_ref,
    own_ref, pre_ref, suf_ref, up_ref, down_ref,
    w_sem, tok_s, tok_r, back_s, back_r, x_s, x_r, c_s, c_r, f_s, f_r, z_s, z_r,
    up_s, up_r, dn_s, dn_r, gx_s, gx_r, gc_s, gc_r, gf_s, gf_r,
):
    tok = tok_ref.shape[0]
    hd = H // nu
    ctx = tok * nu
    bd = ctx // BLOCK
    nz = nb // 4
    half = NGLOBAL // 2
    nj = 2 * hd
    hc = min(2, hd)
    ng = nj // hc
    tb = tok // BLOCK
    b = lax.axis_index("blk")
    u = lax.axis_index("uly")
    r = b % 4
    z = b // 4
    low = r < 2
    inner = (r == 1) | (r == 2)
    has_up = z < nz - 1
    has_dn = z > 0
    px = jnp.where(low, b + 2, b - 2)
    pc = jnp.where(r % 2 == 0, b + 1, b - 1)

    def w_load(part):
        cols = pl.ds(pl.multiple_of(part * H * HD + u * hd * HD, HD), hd * HD)
        return pltpu.make_async_copy(w_ref.at[:, cols], wbuf_ref.at[part], w_sem.at[part])

    for part in (1, 2, 0):
        w_load(part).start()

    barrier = pltpu.get_barrier_semaphore()

    def greet(blk, uly):
        pl.semaphore_signal(
            barrier, inc=1, device_id=(blk, uly), device_id_type=pl.DeviceIdType.MESH
        )

    for d in range(1, nu):
        greet(b, (u + d) % nu)
    greet(px, u)
    greet(pc, u)
    pl.when(has_up)(lambda: greet(b + 4, u))
    pl.when(has_dn)(lambda: greet(b - 4, u))
    pl.semaphore_wait(
        barrier, nu + 1 + jnp.where(has_up, 1, 0) + jnp.where(has_dn, 1, 0)
    )

    def rdma(src, dst, s, rr, blk, uly):
        return pltpu.make_async_remote_copy(
            src_ref=src, dst_ref=dst, send_sem=s, recv_sem=rr,
            device_id=(blk, uly), device_id_type=pl.DeviceIdType.MESH,
        )

    def rows_of(d):
        return ((u + d) % nu) * tok

    def slot(c, s):
        d, g = c // ng, c % ng
        j0 = g % 2 * hd + g // 2 * hc
        return win_ref.at[pl.ds(j0, hc), pl.ds(pl.multiple_of(s * ctx + rows_of(d), tok), tok)]

    def heads_of(g):
        return pl.ds(g % 2 * hd + g // 2 * hc, hc)

    def tok_copy(d):
        return rdma(tok_ref, far_ref.at[d - 1], tok_s.at[d - 1], tok_r.at[d - 1], b, (u + d) % nu)

    for d in range(1, nu):
        tok_copy(d).start()

    def clear(s):
        win_ref[:, pl.ds(s * ctx, ctx), :] = jnp.zeros((nj, ctx, HD), jnp.bfloat16)

    pl.when(b < 2)(lambda: clear(0))
    pl.when(b < 1)(lambda: clear(1))
    pl.when(b > nb - 2)(lambda: clear(3))
    pl.when(b > nb - 3)(lambda: clear(4))

    def project(d, part):
        src = (nu - d) % nu
        toks = tok_ref[...] if src == 0 else far_ref[src - 1]
        res = jnp.dot(toks, wbuf_ref[part], preferred_element_type=jnp.float32)
        res = res.astype(jnp.bfloat16)
        for h in range(hd):
            one = res[:, h * HD:(h + 1) * HD]
            if part == 0:
                q_ref[h, pl.ds(pl.multiple_of(rows_of(d), tok), tok)] = one
            else:
                at = pl.ds(pl.multiple_of(2 * ctx + rows_of(d), tok), tok)
                win_ref[(part - 1) * hd + h, at] = one

    s_x = jnp.where(low, 0, 4)
    s_c = jnp.where(r % 2 == 0, 1, 3)
    in_x = 4 - s_x
    f_src = jnp.where((r == 0) | (r == 2), 4, 0)
    f_dst = jnp.where((r == 0) | (r == 2), 3, 1)

    def x_copy(j):
        return rdma(slot(j, 2), slot(j, s_x), x_s.at[j], x_r.at[j], px, u)

    def c_copy(j):
        return rdma(slot(j, 2), slot(j, s_c), c_s.at[j], c_r.at[j], pc, u)

    def f_copy(j):
        return rdma(slot(j, f_src), slot(j, f_dst), f_s.at[j], f_r.at[j], pc, u)

    z_to = jnp.where(low, b + 4, b - 4)
    z_sends = (low & has_up) | (~low & has_dn)
    z_gets = (low & has_dn) | (~low & has_up)
    f_sends = (r == 0) | (r == 3) | z_gets
    f_gets = inner | z_gets

    def z_copy(j):
        return rdma(slot(j, in_x), slot(j, s_x), z_s.at[j], z_r.at[j], z_to, u)

    def stage_a(c):
        d, g = c // ng, c % ng
        if g == 0 and d > 0:
            tok_copy(nu - d).wait_recv()
        if g < 2:
            if d == 0:
                w_load(1 + g).wait()
            project(d, 1 + g)
        x_copy(c).start()
        c_copy(c).start()
        if g == ng - 1:
            if d == 0:
                w_load(0).wait()
            project(d, 0)

    def stage_b(j):
        x_copy(j).wait_recv()
        pl.when((r == 0) | (r == 3))(lambda: f_copy(j).start())
        pl.when(z_sends)(lambda: z_copy(j).start())

    def stage_c(c):
        @pl.when(z_gets)
        def _():
            z_copy(c).wait_recv()
            pl.when(inner)(lambda: f_copy(c).start())
        c_copy(c).wait_recv()
        pl.when(inner)(lambda: f_copy(c).wait_recv())

    def stage_f(c):
        pl.when(f_gets & ~inner)(lambda: f_copy(c).wait_recv())

    def pick(g0):
        @pl.when(inner)
        def _():
            first = jnp.where(r == 1, 1, 0)
            for g in range(half):
                gid = jnp.where(r == 1, ids_ref[g], ids_ref[half + g]) - 4 * z * bd

                def add(i, acc):
                    at = pl.ds(pl.multiple_of((first * bd + i) * BLOCK, BLOCK), BLOCK)
                    take = jnp.where(gid == i, 1.0, 0.0).astype(jnp.float32)
                    return acc + win_ref[heads_of(g0), at].astype(jnp.float32) * take

                acc = lax.fori_loop(0, 4 * bd, add, jnp.zeros((hc, BLOCK, HD), jnp.float32))
                own_ref[g0, :, g * BLOCK:(g + 1) * BLOCK] = acc.astype(jnp.bfloat16)

    def up_copy(j):
        return rdma(up_ref.at[j], pre_ref.at[j], up_s.at[j], up_r.at[j], b + 4, u)

    def dn_copy(j):
        return rdma(down_ref.at[j], suf_ref.at[j], dn_s.at[j], dn_r.at[j], b - 4, u)

    def wait_in(kind, other, sem_s, sem_r, j):
        rdma(kind.at[j], kind.at[j], sem_s.at[j], sem_r.at[j], other, u).wait_recv()

    def stage_up(j):
        @pl.when(inner)
        def _():
            @pl.when(has_dn)
            def _():
                wait_in(pre_ref, b - 4, up_s, up_r, j)

            @pl.when(~has_dn)
            def _():
                pre_ref[j] = jnp.zeros((hc, half * BLOCK, HD), jnp.bfloat16)

            @pl.when(has_up)
            def _():
                up_ref[j] = pre_ref[j] + own_ref[j]
                up_copy(j).start()

    mine_half = pl.ds(pl.multiple_of(jnp.where(r == 1, 0, half * BLOCK), BLOCK), half * BLOCK)
    fwd_half = pl.ds(pl.multiple_of(jnp.where(r == 0, half * BLOCK, 0), BLOCK), half * BLOCK)

    def gx_copy(j):
        return rdma(glob_ref.at[heads_of(j), mine_half], glob_ref.at[heads_of(j), mine_half],
                    gx_s.at[j], gx_r.at[j], px, u)

    def gc_copy(j):
        return rdma(glob_ref.at[heads_of(j), mine_half], glob_ref.at[heads_of(j), mine_half],
                    gc_s.at[j], gc_r.at[j], pc, u)

    def gf_copy(j):
        return rdma(glob_ref.at[heads_of(j), fwd_half], glob_ref.at[heads_of(j), fwd_half],
                    gf_s.at[j], gf_r.at[j], pc, u)

    def stage_down(j):
        @pl.when(inner)
        def _():
            @pl.when(has_up)
            def _():
                wait_in(suf_ref, b + 4, dn_s, dn_r, j)

            @pl.when(~has_up)
            def _():
                suf_ref[j] = jnp.zeros((hc, half * BLOCK, HD), jnp.bfloat16)

            down_ref[j] = suf_ref[j] + own_ref[j]

            @pl.when(has_dn)
            def _():
                dn_copy(j).start()

    def stage_spread(j):
        @pl.when(inner)
        def _():
            glob_ref[heads_of(j), mine_half] = down_ref[j] + pre_ref[j]
            gx_copy(j).start()
            gc_copy(j).start()

    def stage_out(j):
        @pl.when(~inner)
        def _():
            gx_copy(j).wait_recv()
            gf_copy(j).start()

    reach = REACH * bd
    window = (2 * reach + 1) * BLOCK
    nt = (((1,), (1,)), ((), ()))

    def attend_window(n):
        lb = n % bd
        q_block = b * bd + lb
        key = q_block - reach + lax.broadcasted_iota(jnp.int32, (1, window), 1) // BLOCK
        seen = (jnp.abs(key - q_block) <= band_ref[lb]) & (key >= 0) & (key < nb * bd)
        bias = jnp.where(seen, 0.0, MASKED)
        rows = pl.ds(lb * BLOCK, BLOCK)
        wrows = pl.ds(lb * BLOCK, window)
        for h in range(n // bd * hc, (n // bd + 1) * hc):
            sw = lax.dot_general(
                q_ref[h, rows], win_ref[h, wrows], nt, preferred_element_type=jnp.float32
            )
            sw = sw * EXP2_SCALE + bias
            top = jnp.max(sw, axis=1, keepdims=True)
            pw = jnp.exp2(sw - top)
            top_ref[h, rows] = top
            sum_ref[h, rows] = jnp.sum(pw, axis=1, keepdims=True)
            acc_ref[h, rows] = jnp.dot(
                pw.astype(jnp.bfloat16), win_ref[hd + h, wrows], preferred_element_type=jnp.float32
            )

    def back_copy(k, at_rows, to):
        return rdma(
            att_ref.at[k],
            out_ref.at[pl.ds(pl.multiple_of(at_rows, BLOCK), BLOCK),
                       pl.ds(pl.multiple_of(u * hd * HD, HD), hd * HD)],
            back_s.at[k], back_r.at[k], b, to,
        )

    def finish(k):
        d = k // tb + 1
        to = (u + d) % nu
        lb = to * tb + k % tb
        q_block = b * bd + lb
        lane = lax.broadcasted_iota(jnp.int32, (1, NGLOBAL * BLOCK), 1) // BLOCK
        gid = jnp.zeros_like(lane)
        for g in range(NGLOBAL):
            gid = jnp.where(lane == g, ids_ref[g], gid)
        bias = jnp.where(jnp.abs(gid - q_block) > band_ref[lb], 0.0, MASKED)
        rows = pl.ds(pl.multiple_of(lb * BLOCK, BLOCK), BLOCK)
        for h in range(hd):
            sg = lax.dot_general(
                q_ref[h, rows], glob_ref[h], nt, preferred_element_type=jnp.float32
            )
            sg = sg * EXP2_SCALE + bias
            top = jnp.maximum(top_ref[h, rows], jnp.max(sg, axis=1, keepdims=True))
            pg = jnp.exp2(sg - top)
            old = jnp.exp2(top_ref[h, rows] - top)
            total = sum_ref[h, rows] * old + jnp.sum(pg, axis=1, keepdims=True)
            acc = acc_ref[h, rows] * old + jnp.dot(
                pg.astype(jnp.bfloat16), glob_ref[hd + h], preferred_element_type=jnp.float32
            )
            one = (acc / total).astype(jnp.bfloat16)
            if d < nu:
                att_ref[k, :, h * HD:(h + 1) * HD] = one
            else:
                out_ref[k % tb * BLOCK:(k % tb + 1) * BLOCK,
                        pl.ds(pl.multiple_of((u * hd + h) * HD, HD), HD)] = one
        if d < nu:
            back_copy(k, k % tb * BLOCK, to).start()

    def sweep(j, stage):
        pl.when((j >= 0) & (j < ng))(lambda: stage(j))

    nc = nu * ng
    t0 = nc - ng + 4
    steps = range(t0 + 2, t0 + ng + nz + 1)
    units = hd // hc * bd
    for t in range(t0 + ng + nz + 1):
        for lag, stage in ((0, stage_a), (2, stage_b), (4, stage_c)):
            if 0 <= t - lag < nc:
                stage(t - lag)
        if 0 <= t - t0 < ng:
            pick(t - t0)
        if t >= t0:
            sweep(t - t0 - z, stage_up)
            sweep(t - t0 - (nz - 1 - z), stage_down)
        for lag, stage in ((t0 + nz, stage_spread), (t0 + nz + 1, stage_out)):
            if 0 <= t - lag < ng:
                stage(t - lag)
        if 0 <= t - 5 < nc:
            stage_f(t - 5)
        for n in range(units):
            if t == max(steps[n * len(steps) // units], t0 + 2 + n // bd * 2):
                attend_window(n)

    for j in range(ng):
        pl.when(inner)(lambda: gf_copy(j).wait_recv())
        pl.when(~inner)(lambda: gc_copy(j).wait_recv())
    for k in range(bd):
        finish(k)

    for d in range(1, nu):
        tok_copy(d).wait_send()
    for c in range(nc):
        x_copy(c).wait_send()
        c_copy(c).wait_send()
        pl.when(f_sends)(lambda: f_copy(c).wait_send())
        pl.when(z_sends)(lambda: z_copy(c).wait_send())
    for j in range(ng):
        @pl.when(inner)
        def _():
            pl.when(has_up)(lambda: up_copy(j).wait_send())
            pl.when(has_dn)(lambda: dn_copy(j).wait_send())
            gx_copy(j).wait_send()
            gc_copy(j).wait_send()

        pl.when(~inner)(lambda: gf_copy(j).wait_send())
    for k in range(bd - tb):
        back_copy(k, k % tb * BLOCK, (u + k // tb + 1) % nu).wait()


def layer(nb, nu, band, global_ids, tokens, w_qkv):
    tok, width = tokens.shape
    hd = H // nu
    ctx = tok * nu
    bd = ctx // BLOCK
    nj = 2 * hd
    hc = min(2, hd)
    ng = nj // hc
    back = bd - tok // BLOCK
    share = pltpu.VMEM((ng, hc, NGLOBAL // 2 * BLOCK, HD), jnp.bfloat16)
    dma = pltpu.SemaphoreType.DMA
    smem = pl.BlockSpec(memory_space=pltpu.SMEM)
    vmem = pl.BlockSpec(memory_space=pltpu.VMEM)
    return pl.pallas_call(
        functools.partial(layer_kernel, nb, nu),
        out_shape=jax.ShapeDtypeStruct((tok, H * HD), jnp.bfloat16),
        in_specs=[smem, smem, vmem, pl.BlockSpec(memory_space=pl.ANY)],
        out_specs=vmem,
        scratch_shapes=[
            pltpu.VMEM((hd, ctx, HD), jnp.bfloat16),
            pltpu.VMEM((nj, SLOTS * ctx, HD), jnp.bfloat16),
            pltpu.VMEM((nj, NGLOBAL * BLOCK, HD), jnp.bfloat16),
            pltpu.VMEM((nu - 1, tok, width), jnp.bfloat16),
            pltpu.VMEM((3, width, hd * HD), jnp.bfloat16),
            pltpu.VMEM((hd, ctx, HD), jnp.float32),
            pltpu.VMEM((hd, ctx, 1), jnp.float32),
            pltpu.VMEM((hd, ctx, 1), jnp.float32),
            pltpu.VMEM((back, BLOCK, hd * HD), jnp.bfloat16),
            share, share, share, share, share,
            dma((3,)), dma((nu - 1,)), dma((nu - 1,)), dma((back,)), dma((back,)),
        ] + [dma((nu * ng,))] * 8 + [dma((ng,))] * 10,
        compiler_params=pltpu.CompilerParams(
            collective_id=0, has_side_effects=True, vmem_limit_bytes=VMEM_LIMIT
        ),
    )(band, global_ids, tokens, w_qkv)


def body(nb, nu, tokens, w_qkv, w_out, band, global_ids):
    attended = layer(nb, nu, band, global_ids, tokens, w_qkv)
    result = jnp.dot(attended, w_out, preferred_element_type=jnp.float32)
    return result.astype(jnp.bfloat16)


def solution(mesh):
    return jax.shard_map(
        functools.partial(body, mesh.shape["blk"], mesh.shape["uly"]),
        mesh=mesh,
        in_specs=(P(("blk", "uly"), None), P(), P(), P("blk"), P()),
        out_specs=P(("blk", "uly"), None),
        check_vma=False,
    )
```

time: 94.1 us -> 76.8 us (0.82)
  blocking collectives: 11.5 us -> 0 us
  Pallas kernels: 79.6 us -> 74.1 us
  local copies, waits for them, and re-layouts: 1.25 us -> 0.01 us
  matrix products: 1.52 us -> 2.55 us
    all_to_all x1 -> x0, blocking collectives: 11.5 us -> none  [body(): lax.all_to_all(attended, 'uly', split_axis=0, concat_axis=1, tiled=True)]
    pallas_call x2 -> x1, Pallas kernels: 79.6 us -> 74.1 us  [layer(): pl.pallas_call(functools.partial(layer_kernel, nb, nu), out_shape=jax.Sha...]
    all_to_all x1 -> x0, local copies, waits for them, and re-layouts: 1.24 us -> none  [body(): lax.all_to_all(attended, 'uly', split_axis=0, concat_axis=1, tiled=True)]
    dot_general x1, matrix products: 1.52 us -> 2.55 us  [body(): result = jnp.dot(attended, w_out, preferred_element_type=jnp.float32)]
where the time goes in v3:
time: 76.8 us; the launch traced here: 76.7 us
  Pallas kernels  74.1 us (96%)
  matrix products  2.55 us (3%)
    pallas_call x1, Pallas kernels, layer(): pl.pallas_call(functools.partial(layer_kernel, nb, nu), out_shape=jax.Sha...  74.1 us
    dot_general x1, matrix products, body(): result = jnp.dot(attended, w_out, preferred_element_type=jnp.float32)  2.55 us

profile of v3, /device:TPU:0, one launch (start us, length us, event | category | flops | bytes accessed | tf_op | source)
XLA Modules:
  0.0 76.7 jit_solution(2757598202330272407)
XLA Ops:
  0.0 0.0 copy-start
  0.0 74.1 %shard_map.55 = bf16[256,1024]{1,0:T(8,128)(2,1)} custom-call(s32[4]{0:T(128)} %band_ref.1, s32[4]{0:T(128)} %ids_ref.1, bf16[256,1024]{1,0:T(8,128)(2,1)} %tok_ref.1, bf16[1024,3072]{1,0:T(8,128)(2,1)} %w_ref.1), custom_call_target="tpu_custom_call" | custom-call | tf_op jit(solution)/shard_map/pallas_call | solution.py:387
  74.1 0.0 copy-done
  74.1 2.5 %convolution_convert_fusion = bf16[256,1024]{1,0:T(8,128)(2,1)} fusion(bf16[256,1024]{1,0:T(8,128)(2,1)} %shard_map.55, bf16[1024,1024]{1,0:T(8,128)(2,1)S(1)} %copy-done), kind=kOutput, calls=%fused_computation | convolution fusion | flops 537133056 | bytes 3145728 | tf_op jit(solution)/shard_map/dot_general | solution.py:413
Async XLA Ops:
  0.0 74.1 %copy-start = (bf16[1024,1024]{1,0:T(8,128)(2,1)S(1)}, bf16[1024,1024]{1,0:T(8,128)(2,1)}, u32[]{:S(2)}) copy-start(bf16[1024,1024]{1,0:T(8,128)(2,1)} %param.7) | copy-start | bytes 6291460
